TPU v7x, 32 devices: a whole 2x2x4 slice. The times are simulated.
32 devices in a mesh: fsdp: 2 (over y), ctx: 4 (over x, core), tensor: 4 (over z).
Axes of the slice: x: 2, y: 2, z: 4, core: 2. Of those that a mesh axis runs over, the one named last changes fastest.
Arguments:
- latents_in: bfloat16 [6, 1024, 768], P('fsdp', 'ctx'), may hold values from -6 to 6
- conditioning: bfloat16 [6, 768], P('fsdp'), may hold values from -6 to 6
- ada_weight: bfloat16 [768, 6, 768], P(('fsdp', 'ctx'), None, 'tensor'), may hold values from -0.21875 to 0.21875
- ada_bias: bfloat16 [6, 768], P(None, ('tensor', 'fsdp', 'ctx')), may hold values from -3 to 3
- qkv_weight: bfloat16 [768, 3, 768], P(('fsdp', 'ctx'), None, 'tensor'), may hold values from -0.21875 to 0.21875
- qv_bias: bfloat16 [2, 768], P(None, ('tensor', 'fsdp', 'ctx')), may hold values from -3 to 3
- out_weight: bfloat16 [768, 768], P('tensor', ('fsdp', 'ctx')), may hold values from -1.75 to 1.75
- out_bias: bfloat16 [768], P(('fsdp', 'ctx')), may hold values from -3 to 3
- up_weight: bfloat16 [768, 3072], P(('fsdp', 'ctx'), 'tensor'), may hold values from -0.21875 to 0.21875
- up_bias: bfloat16 [3072], P(('tensor', 'fsdp', 'ctx')), may hold values from -3 to 3
- down_weight: bfloat16 [3072, 768], P('tensor', ('fsdp', 'ctx')), may hold values from -0.109375 to 0.109375
- down_bias: bfloat16 [768], P(('fsdp', 'ctx')), may hold values from -3 to 3
- cotangent: bfloat16 [6, 1024, 768], P('fsdp', 'ctx'), may hold values from -6 to 6
Outputs:
- block_out: bfloat16 [6, 1024, 768], P('fsdp', 'ctx')
- grad_in: float32 [6, 1024, 768], P('fsdp', 'ctx')
- grad_cond: float32 [6, 768], P('fsdp')
- grad_ada_weight: float32 [768, 6, 768], P(('fsdp', 'ctx'), None, 'tensor')
- grad_ada_bias: float32 [6, 768], P(None, ('tensor', 'fsdp', 'ctx'))
- grad_qkv_weight: float32 [768, 3, 768], P(('fsdp', 'ctx'), None, 'tensor')
- grad_qv_bias: float32 [2, 768], P(None, ('tensor', 'fsdp', 'ctx'))
- grad_out_weight: float32 [768, 768], P('tensor', ('fsdp', 'ctx'))
- grad_out_bias: float32 [768], P(('fsdp', 'ctx'))
- grad_up_weight: float32 [768, 3072], P(('fsdp', 'ctx'), 'tensor')
- grad_up_bias: float32 [3072], P(('tensor', 'fsdp', 'ctx'))
- grad_down_weight: float32 [3072, 768], P('tensor', ('fsdp', 'ctx'))
- grad_down_bias: float32 [768], P(('fsdp', 'ctx'))
All inputs are finite; a program needn't handle non-finite values.
Results may differ from a plain program's by a relative error of at most 0.017.
Values may be sent and summed in bfloat16 or wider, within the bound.
A program may use at most 128 MiB of HBM per device.

v0:
```python
import math

import jax
import jax.numpy as jnp
from jax import lax
from jax.sharding import PartitionSpec as P

HEAD_DIM = 64


EPSILON = 1e-06
GELU_SCALE = 0.7978845608028654
GELU_CUBIC = 0.044715


def layer_norm(values):
    center = values - jnp.mean(values, axis=-1, keepdims=True)
    spread = jnp.mean(center * center, axis=-1, keepdims=True)
    return center * lax.rsqrt(spread + EPSILON)


def gelu_tanh(pre_act):
    return (
        0.5
        * pre_act
        * (1.0 + jnp.tanh(GELU_SCALE * (pre_act + GELU_CUBIC * pre_act * pre_act * pre_act)))
    )


def silu_slope(values):
    sigmoid_val = jax.nn.sigmoid(values)
    return sigmoid_val * (1.0 + values * (1.0 - sigmoid_val))


def body(
    latents_in,
    conditioning,
    ada_weight,
    ada_bias,
    qkv_weight,
    qv_bias,
    out_weight,
    out_bias,
    up_weight,
    up_bias,
    down_weight,
    down_bias,
    cotangent,
):
    gathered = (
        lax.all_gather(ada_weight, ("fsdp", "ctx"), axis=0, tiled=True),
        lax.all_gather(qkv_weight, ("fsdp", "ctx"), axis=0, tiled=True),
        lax.all_gather(up_weight, ("fsdp", "ctx"), axis=0, tiled=True),
        lax.all_gather(out_weight, ("fsdp", "ctx"), axis=1, tiled=True),
        lax.all_gather(down_weight, ("fsdp", "ctx"), axis=1, tiled=True),
        lax.all_gather(ada_bias, ("fsdp", "ctx"), axis=1, tiled=True),
        lax.all_gather(qv_bias, ("fsdp", "ctx"), axis=1, tiled=True),
        lax.all_gather(out_bias, ("fsdp", "ctx"), axis=0, tiled=True),
        lax.all_gather(up_bias, ("fsdp", "ctx"), axis=0, tiled=True),
        lax.all_gather(down_bias, ("fsdp", "ctx"), axis=0, tiled=True),
    )
    ada_full, qkv_full, up_full, out_full, down_full = (
        gathered[0],
        gathered[1],
        gathered[2],
        gathered[3],
        gathered[4],
    )
    ada_shift, qv_shift, out_shift, up_shift, down_shift = (
        gathered[5],
        gathered[6],
        gathered[7],
        gathered[8],
        gathered[9],
    )
    latent_count, tok_rows = (latents_in.shape[0], latents_in.shape[1])
    part_width = qkv_full.shape[2]
    local_heads = part_width // HEAD_DIM
    score_scale = 1.0 / math.sqrt(HEAD_DIM)
    lifted = jax.nn.silu(conditioning.astype(jnp.float32))
    lifted_low = lifted.astype(jnp.bfloat16)
    mod_part = jnp.einsum(
        "bd,dje->bje", lifted_low, ada_full, preferred_element_type=jnp.float32
    ) + ada_shift.astype(jnp.float32)
    modulation = lax.all_gather(mod_part, "tensor", axis=2, tiled=True)
    shift_one, scale_one, gate_one, shift_two, scale_two, gate_two = [
        modulation[:, offset][:, None, :] for offset in range(6)
    ]
    inputs = latents_in.astype(jnp.float32)
    normed, norm_back = jax.vjp(layer_norm, inputs)
    shifted = (normed * (1.0 + scale_one) + shift_one).astype(jnp.bfloat16)
    project = jnp.einsum("bld,dje->blje", shifted, qkv_full, preferred_element_type=jnp.float32)
    queries = (project[:, :, 0] + qv_shift[0].astype(jnp.float32)).astype(jnp.bfloat16)
    key_part = project[:, :, 1].astype(jnp.bfloat16)
    value_part = (project[:, :, 2] + qv_shift[1].astype(jnp.float32)).astype(jnp.bfloat16)
    key_all, value_all = (
        lax.all_gather(key_part, "ctx", axis=1, tiled=True),
        lax.all_gather(value_part, "ctx", axis=1, tiled=True),
    )
    seq_len = key_all.shape[1]
    query_heads = queries.reshape(latent_count, tok_rows, local_heads, HEAD_DIM)
    key_heads = key_all.reshape(latent_count, seq_len, local_heads, HEAD_DIM)
    value_heads = value_all.reshape(latent_count, seq_len, local_heads, HEAD_DIM)
    scores = (
        jnp.einsum("bqhe,bkhe->bhqk", query_heads, key_heads, preferred_element_type=jnp.float32)
        * score_scale
    )
    log_total = jax.nn.logsumexp(scores, axis=-1, keepdims=True)
    prob_low = jnp.exp(scores - log_total).astype(jnp.bfloat16)
    mixed_heads = (
        jnp.einsum("bhqk,bkhe->bqhe", prob_low, value_heads, preferred_element_type=jnp.float32)
        .astype(jnp.bfloat16)
        .reshape(latent_count, tok_rows, part_width)
    )
    attn_part = jnp.einsum("bld,de->ble", mixed_heads, out_full, preferred_element_type=jnp.float32)
    attended = lax.psum(attn_part.astype(jnp.bfloat16), "tensor").astype(
        jnp.float32
    ) + out_shift.astype(jnp.float32)
    after_attn = inputs + gate_one * attended
    normed_two, norm_back_two = jax.vjp(layer_norm, after_attn)
    shifted_two = (normed_two * (1.0 + scale_two) + shift_two).astype(jnp.bfloat16)
    hidden_pre = jnp.einsum(
        "bld,df->blf", shifted_two, up_full, preferred_element_type=jnp.float32
    ) + up_shift.astype(jnp.float32)
    hidden_val, gelu_back = jax.vjp(gelu_tanh, hidden_pre)
    hidden = hidden_val.astype(jnp.bfloat16)
    feed_part = jnp.einsum("blf,fd->bld", hidden, down_full, preferred_element_type=jnp.float32)
    feed_out = lax.psum(feed_part.astype(jnp.bfloat16), "tensor").astype(
        jnp.float32
    ) + down_shift.astype(jnp.float32)
    block_out = (after_attn + gate_two * feed_out).astype(jnp.bfloat16)
    again = (
        lax.all_gather(ada_weight, ("fsdp", "ctx"), axis=0, tiled=True),
        lax.all_gather(qkv_weight, ("fsdp", "ctx"), axis=0, tiled=True),
        lax.all_gather(up_weight, ("fsdp", "ctx"), axis=0, tiled=True),
        lax.all_gather(out_weight, ("fsdp", "ctx"), axis=1, tiled=True),
        lax.all_gather(down_weight, ("fsdp", "ctx"), axis=1, tiled=True),
    )
    ada_back, qkv_back, up_back, out_back, down_back = (
        again[0],
        again[1],
        again[2],
        again[3],
        again[4],
    )
    upstream = cotangent.astype(jnp.float32)
    feed_grad = (gate_two * upstream).astype(jnp.bfloat16)
    gate_two_grad = jnp.sum(upstream * feed_out, axis=1)
    down_bias_grad = jnp.sum(feed_grad.astype(jnp.float32), axis=(0, 1))
    down_weight_grad = jnp.einsum(
        "blf,bld->fd", hidden, feed_grad, preferred_element_type=jnp.float32
    )
    hidden_grad = jnp.einsum(
        "bld,fd->blf", feed_grad, down_back, preferred_element_type=jnp.float32
    )
    pre_grad = gelu_back(hidden_grad)[0].astype(jnp.bfloat16)
    up_bias_grad = jnp.sum(pre_grad.astype(jnp.float32), axis=(0, 1))
    up_weight_grad = jnp.einsum(
        "bld,blf->df", shifted_two, pre_grad, preferred_element_type=jnp.float32
    )
    two_part = jnp.einsum("blf,df->bld", pre_grad, up_back, preferred_element_type=jnp.float32)
    shifted_two_grad = lax.psum(two_part.astype(jnp.bfloat16), "tensor").astype(jnp.float32)
    scale_two_grad = jnp.sum(shifted_two_grad * normed_two, axis=1)
    shift_two_grad = jnp.sum(shifted_two_grad, axis=1)
    after_grad = upstream + norm_back_two(shifted_two_grad * (1.0 + scale_two))[0]
    attn_grad = (gate_one * after_grad).astype(jnp.bfloat16)
    gate_one_grad = jnp.sum(after_grad * attended, axis=1)
    out_bias_grad = jnp.sum(attn_grad.astype(jnp.float32), axis=(0, 1))
    out_weight_grad = jnp.einsum(
        "bld,ble->de", mixed_heads, attn_grad, preferred_element_type=jnp.float32
    )
    mixed_grad = jnp.einsum(
        "ble,de->bld", attn_grad, out_back, preferred_element_type=jnp.float32
    ).astype(jnp.bfloat16)
    mixed_grad = mixed_grad.reshape(latent_count, tok_rows, local_heads, HEAD_DIM)
    scores_again = (
        jnp.einsum("bqhe,bkhe->bhqk", query_heads, key_heads, preferred_element_type=jnp.float32)
        * score_scale
    )
    probs = jnp.exp(scores_again - log_total)
    prob_grad = jnp.einsum(
        "bqhe,bkhe->bhqk", mixed_grad, value_heads, preferred_element_type=jnp.float32
    )
    row_term = jnp.sum(probs * prob_grad, axis=-1, keepdims=True)
    score_grad = (probs * (prob_grad - row_term)).astype(jnp.bfloat16)
    query_grad = (
        jnp.einsum("bhqk,bkhe->bqhe", score_grad, key_heads, preferred_element_type=jnp.float32)
        * score_scale
    ).astype(jnp.bfloat16)
    query_grad = query_grad.reshape(latent_count, tok_rows, part_width)
    probs_again = probs.astype(jnp.bfloat16)
    key_term = (
        jnp.einsum("bhqk,bqhe->bkhe", score_grad, query_heads, preferred_element_type=jnp.float32)
        * score_scale
    ).reshape(latent_count, seq_len, part_width)
    value_term = jnp.einsum(
        "bhqk,bqhe->bkhe", probs_again, mixed_grad, preferred_element_type=jnp.float32
    ).reshape(latent_count, seq_len, part_width)
    key_sum, value_sum = (
        lax.psum_scatter(
            key_term.astype(jnp.bfloat16), "ctx", scatter_dimension=1, tiled=True
        ).astype(jnp.float32),
        lax.psum_scatter(
            value_term.astype(jnp.bfloat16), "ctx", scatter_dimension=1, tiled=True
        ).astype(jnp.float32),
    )
    key_grad = key_sum.astype(jnp.bfloat16)
    value_grad = value_sum.astype(jnp.bfloat16)
    qv_bias_grad = jnp.stack(
        [
            jnp.sum(query_grad.astype(jnp.float32), axis=(0, 1)),
            jnp.sum(value_grad.astype(jnp.float32), axis=(0, 1)),
        ]
    )
    proj_grad = jnp.stack([query_grad, key_grad, value_grad], axis=2)
    qkv_weight_grad = jnp.einsum(
        "bld,blje->dje", shifted, proj_grad, preferred_element_type=jnp.float32
    )
    one_part = jnp.einsum("blje,dje->bld", proj_grad, qkv_back, preferred_element_type=jnp.float32)
    shifted_grad = lax.psum(one_part.astype(jnp.bfloat16), "tensor").astype(jnp.float32)
    scale_one_grad = jnp.sum(shifted_grad * normed, axis=1)
    shift_one_grad = jnp.sum(shifted_grad, axis=1)
    grad_in = after_grad + norm_back(shifted_grad * (1.0 + scale_one))[0]
    mod_grad_full = jnp.stack(
        [
            shift_one_grad,
            scale_one_grad,
            gate_one_grad,
            shift_two_grad,
            scale_two_grad,
            gate_two_grad,
        ],
        axis=1,
    )
    column = lax.axis_index("tensor") * part_width
    mod_grad_part = lax.dynamic_slice_in_dim(mod_grad_full, column, part_width, 2)
    mod_grad = lax.psum(mod_grad_part, "ctx").astype(jnp.bfloat16)
    owner_mask = (lax.axis_index("ctx") == 0).astype(jnp.float32)
    ada_bias_grad = jnp.sum(mod_grad.astype(jnp.float32), axis=0) * owner_mask
    ada_weight_grad = (
        jnp.einsum("bd,bje->dje", lifted_low, mod_grad, preferred_element_type=jnp.float32)
        * owner_mask
    )
    lifted_part = jnp.einsum("bje,dje->bd", mod_grad, ada_back, preferred_element_type=jnp.float32)
    lifted_grad = lax.psum(lifted_part, "tensor")
    grad_cond = lifted_grad * silu_slope(conditioning.astype(jnp.float32))
    shards = (
        lax.psum_scatter(ada_weight_grad, ("fsdp", "ctx"), scatter_dimension=0, tiled=True),
        lax.psum_scatter(qkv_weight_grad, ("fsdp", "ctx"), scatter_dimension=0, tiled=True),
        lax.psum_scatter(up_weight_grad, ("fsdp", "ctx"), scatter_dimension=0, tiled=True),
        lax.psum_scatter(out_weight_grad, ("fsdp", "ctx"), scatter_dimension=1, tiled=True),
        lax.psum_scatter(down_weight_grad, ("fsdp", "ctx"), scatter_dimension=1, tiled=True),
        lax.psum_scatter(ada_bias_grad, ("fsdp", "ctx"), scatter_dimension=1, tiled=True),
        lax.psum_scatter(qv_bias_grad, ("fsdp", "ctx"), scatter_dimension=1, tiled=True),
        lax.psum_scatter(out_bias_grad, ("fsdp", "ctx"), scatter_dimension=0, tiled=True),
        lax.psum_scatter(up_bias_grad, ("fsdp", "ctx"), scatter_dimension=0, tiled=True),
        lax.psum_scatter(down_bias_grad, ("fsdp", "ctx"), scatter_dimension=0, tiled=True),
    )
    return (
        block_out,
        grad_in,
        grad_cond,
        shards[0],
        shards[5],
        shards[1],
        shards[6],
        shards[3],
        shards[7],
        shards[2],
        shards[8],
        shards[4],
        shards[9],
    )


def solution(mesh):
    in_specs = (
        P("fsdp", "ctx", None),
        P("fsdp", None),
        P(("fsdp", "ctx"), None, "tensor"),
        P(None, ("tensor", "fsdp", "ctx")),
        P(("fsdp", "ctx"), None, "tensor"),
        P(None, ("tensor", "fsdp", "ctx")),
        P("tensor", ("fsdp", "ctx")),
        P(("fsdp", "ctx")),
        P(("fsdp", "ctx"), "tensor"),
        P(("tensor", "fsdp", "ctx")),
        P("tensor", ("fsdp", "ctx")),
        P(("fsdp", "ctx")),
        P("fsdp", "ctx", None),
    )
    out_specs = (
        P("fsdp", "ctx", None),
        P("fsdp", "ctx", None),
        P("fsdp", None),
        P(("fsdp", "ctx"), None, "tensor"),
        P(None, ("tensor", "fsdp", "ctx")),
        P(("fsdp", "ctx"), None, "tensor"),
        P(None, ("tensor", "fsdp", "ctx")),
        P("tensor", ("fsdp", "ctx")),
        P(("fsdp", "ctx")),
        P(("fsdp", "ctx"), "tensor"),
        P(("tensor", "fsdp", "ctx")),
        P("tensor", ("fsdp", "ctx")),
        P(("fsdp", "ctx")),
    )
    return jax.shard_map(body, mesh=mesh, in_specs=in_specs, out_specs=out_specs, check_vma=False)
```

profile of v0, /device:TPU:0, one launch (start us, length us, event | category | flops | bytes accessed | tf_op | source)
XLA Modules:
  0.0 717.6 jit_solution(5319754886577921093)
XLA Ops:
  8.0 10.6 %all-gather.1 = bf16[8,24,6]{1,2,0:T(8,128)(2,1)S(1)} all-gather(bf16[1,24,6]{1,2,0:T(8,128)(2,1)} %bitcast.194), channel_id=1, replica_groups=mesh['fsdp'=2,'ctx'=4,'tensor'=4] {'fsdp','ctx'}, dimensions={0}, use_global_device_ids=true | all-gather | bytes 2592 | tf_op jit(solution)/shard_map/all_gather | solution.py:56
  19.7 16.4 %all_gather.47 = bf16[768,3,192]{2,1,0:T(4,128)(2,1)} all-gather(bf16[96,3,192]{2,1,0:T(4,128)(2,1)S(1)} %copy.87), channel_id=1, replica_groups=mesh['fsdp'=2,'ctx'=4,'tensor'=4] {'fsdp','ctx'}, dimensions={0}, use_global_device_ids=true | all-gather | bytes 995328 | tf_op jit(solution)/shard_map/all_gather | solution.py:52
  36.1 2.6 copy.88
  39.4 4.1 all-gather.9.cloned.1.call-done
  43.5 2.1 convolution_add_fusion
  45.8 30.1 %all_gather.46 = f32[3,6,768]{1,0,2:T(4,128)S(1)} all-gather(f32[3,6,192]{1,0,2:T(4,128)S(1)} %copy.83), channel_id=1, replica_groups=mesh['fsdp'=2,'ctx'=4,'tensor'=4] {'tensor'}, dimensions={2}, use_global_device_ids=true | all-gather | bytes 69120 | tf_op jit(solution)/shard_map/all_gather | solution.py:85
  75.9 6.4 fusion.70
  82.3 1.6 copy.123
  83.9 1.7 copy.86
  88.7 8.7 %all-gather.2 = bf16[8,24,2]{1,2,0:T(2,128)(2,1)S(1)} all-gather(bf16[1,24,2]{1,2,0:T(2,128)(2,1)S(1)} %bitcast.195), channel_id=1, replica_groups=mesh['fsdp'=2,'ctx'=4,'tensor'=4] {'fsdp','ctx'}, dimensions={0}, use_global_device_ids=true | all-gather | bytes 864 | tf_op jit(solution)/shard_map/all_gather | solution.py:57
  97.5 1.9 fusion.42
  99.7 9.2 %all_gather.51 = bf16[192,768]{0,1:T(8,128)(2,1)S(1)} all-gather(bf16[192,96]{0,1:T(8,128)(2,1)S(1)} %copy.90), channel_id=1, replica_groups=mesh['fsdp'=2,'ctx'=4,'tensor'=4] {'fsdp','ctx'}, dimensions={1}, use_global_device_ids=true | all-gather | bytes 331776 | tf_op jit(solution)/shard_map/all_gather | solution.py:54
  110.2 3.0 multiply_reduce_fusion.1
  113.3 1.9 exponential_reduce_fusion
  115.2 1.7 copy-done
  116.9 10.2 %all-gather.11.cloned.1.call-done = bf16[3,1024,192]{1,2,0:T(8,128)(2,1)} async-done(((bf16[3,256,192]{1,2,0:T(8,128)(2,1)}), bf16[3,1024,192]{1,2,0:T(8,128)(2,1)}) %all-gather.11.cloned.1.call-update) | async-done | bytes 1179664 | tf_op jit(solution)/shard_map/all_gather | solution.py:98
  127.2 5.9 convolution_convert_fusion.4
  133.1 1.5 convolution_convert_fusion.3
  138.1 14.2 %all-reduce.9 = (bf16[768]{0:T(1024)(128)(2,1)S(1)}, bf16[768]{0:T(1024)(128)(2,1)S(1)}, bf16[768]{0:T(1024)(128)(2,1)}) all-reduce(bf16[768]{0:T(1024)(128)(2,1)S(1)} %dynamic-update-slice, bf16[768]{0:T(1024)(128)(2,1)S(1)} %dynamic-update-slice.1, ...), channel_id=1, replica_groups=mesh['fsdp'=2,'ctx'=4,'tensor'=4] {'fsdp','ctx'}, use_global_device_ids=true, to_apply=%add | all-reduce | flops 2304 | bytes 9216
  152.9 2.3 copy.92
  155.2 1.6 copy.124
  157.4 2.3 copy.94
  159.6 1.7 copy.84
  161.3 29.5 %all-reduce.15.cloned.1.call-done = bf16[3,256,768]{2,1,0:T(8,128)(2,1)} async-done(((bf16[3,256,768]{2,1,0:T(8,128)(2,1)}), bf16[3,256,768]{2,1,0:T(8,128)(2,1)}) %all-reduce.15.cloned.1.call-update) | async-done | bytes 1179664 | tf_op jit(solution)/shard_map/psum | solution.py:116
  190.8 1.9 fusion.69
  195.2 21.0 %all-gather.13.cloned.1.call-done = bf16[768,768]{1,0:T(8,128)(2,1)} async-done(((bf16[96,768]{1,0:T(8,128)(2,1)}), bf16[768,768]{1,0:T(8,128)(2,1)}) %all-gather.13.cloned.1.call-update) | async-done | bytes 1179664 | tf_op jit(solution)/shard_map/all_gather | solution.py:53
  216.1 4.4 fusion.31
  220.5 21.5 %all-gather.15.cloned.1.call-done = bf16[768,768]{0,1:T(8,128)(2,1)} async-done(((bf16[768,96]{0,1:T(8,128)(2,1)}), bf16[768,768]{0,1:T(8,128)(2,1)}) %all-gather.15.cloned.1.call-update) | async-done | bytes 1179664 | tf_op jit(solution)/shard_map/all_gather | solution.py:55
  242.0 5.1 convert_reduce_fusion.4
  248.1 2.1 convolution_convert_fusion.1
  250.3 56.0 %all-reduce.17.cloned.1.call-done = bf16[3,256,768]{2,1,0:T(8,128)(2,1)} async-done(((bf16[3,256,768]{2,1,0:T(8,128)(2,1)}), bf16[3,256,768]{2,1,0:T(8,128)(2,1)}) %all-reduce.17.cloned.1.call-update) | async-done | bytes 1179664 | tf_op jit(solution)/shard_map/psum | solution.py:162
  306.3 2.3 fusion.11
  309.4 1.9 fusion.34
  311.5 2.1 convert_reduce_fusion.5
  315.2 6.6 convolution_convert_fusion
  322.1 7.0 multiply_reduce_fusion
  329.1 5.6 multiply_convert_fusion
  334.8 2.5 multiply_convert_fusion.1
  337.4 4.8 convolution_convert_fusion.2
  342.2 2.9 convert_reduce_fusion.7
  345.1 2.2 reduce-scatter.14.cloned.1.call-done
  347.3 28.5 %reduce-scatter.12.cloned.1.call-done = bf16[3,256,192]{1,2,0:T(8,128)(2,1)} async-done(((bf16[3,1024,192]{1,2,0:T(8,128)(2,1)}), bf16[3,256,192]{1,2,0:T(8,128)(2,1)}) %reduce-scatter.12.cloned.1.call-update) | async-done | bytes 294928 | tf_op jit(solution)/shard_map/reduce_scatter | solution.py:200
  375.8 3.9 bitcast_convert_fusion
  379.7 2.9 convolution_bitcast_fusion.3
  382.7 5.0 convolution_bitcast_fusion.1
  387.7 4.3 convolution_bitcast_fusion.2
  393.5 4.1 convolution_bitcast_fusion
  397.8 78.1 %all-reduce.19.cloned.1.call-done = (bf16[3,256,768]{2,1,0:T(8,128)(2,1)}, bf16[3,256,768]{2,1,0:T(8,128)(2,1)}) async-done(((bf16[3,256,768]{2,1,0:T(8,128)(2,1)}, bf16[3,256,768]{2,1,0:T(8,128)(2,1)}), (bf16[3,256,768]{2,1,0:T(8,128)(2,1)}, bf16[3,256,768]{2,1,0:T(8,128)(2,1)})) %all-reduce.19.cloned.1.call-update) | async-done | bytes 2359312 | tf_op jit(solution)/shard_map/psum | solution.py:128
  475.9 2.1 fusion.17
  478.7 6.8 fusion.22
  486.2 12.6 %psum.46 = bf16[3,6,192]{2,0,1:T(4,128)(2,1)} all-reduce(f32[3,6,192]{2,0,1:T(4,128)} %constant_dynamic-slice_fusion.2), channel_id=1, replica_groups=mesh['fsdp'=2,'ctx'=4,'tensor'=4] {'ctx'}, use_global_device_ids=true, to_apply=%region_23.24 | all-reduce | flops 3456 | bytes 20736 | tf_op jit(solution)/shard_map/psum | solution.py:237
  498.8 3.7 broadcast_multiply_fusion
  503.8 1.3 stack.49
  505.1 7.9 %reduce-scatter.24.cloned.1.call-done = f32[96,192]{1,0:T(8,128)} async-done(((f32[768,192]{1,0:T(8,128)}), f32[96,192]{1,0:T(8,128)}) %reduce-scatter.24.cloned.1.call-update) | async-done | bytes 73744
  513.1 1.6 copy.118
  518.4 24.1 %all-reduce.8 = (f32[6,192]{1,0:T(8,128)}, f32[2,192]{1,0:T(2,128)}, f32[768]{0:T(1024)}, f32[768]{0:T(1024)}, f32[768]{0:T(1024)}) all-reduce(f32[6,192]{1,0:T(8,128)} %broadcast_multiply_fusion.1, f32[2,192]{1,0:T(2,128)} %pad_maximum_fusion.3, ...), channel_id=6, replica_groups=mesh['fsdp'=2,'ctx'=4,'tensor'=4] {'fsdp','ctx'}, use_global_device_ids=true, to_apply=%region_27.28.clone | all-reduce | flops 3840 | bytes 30720
  546.3 3.0 convolution_bitcast_fusion.4
  549.3 19.9 %psum.47 = f32[3,768]{1,0:T(4,128)} all-reduce(f32[3,768]{1,0:T(4,128)} %convolution_bitcast_fusion.4), channel_id=1, replica_groups=mesh['fsdp'=2,'ctx'=4,'tensor'=4] {'tensor'}, use_global_device_ids=true, to_apply=%region_24.25 | all-reduce | flops 2304 | bytes 18432 | tf_op jit(solution)/shard_map/psum | solution.py:245
  570.6 1.4 constant_dynamic-slice_fusion.1
  572.6 1.3 fusion.54
  574.0 4.9 add_add_fusion.2
  578.9 27.3 %reduce-scatter.20.cloned.1.call-done = f32[96,768]{1,0:T(8,128)} async-done(((f32[768,768]{1,0:T(8,128)}), f32[96,768]{1,0:T(8,128)}) %reduce-scatter.20.cloned.1.call-update) | async-done | bytes 294928 | tf_op jit(solution)/shard_map/reduce_scatter | solution.py:250
  606.2 46.3 %reduce-scatter.18.cloned.1.call-done = f32[96,3,192]{2,0,1:T(8,128)} async-done(((f32[768,3,192]{2,0,1:T(8,128)}), f32[96,3,192]{2,0,1:T(8,128)}) %reduce-scatter.18.cloned.1.call-update) | async-done | bytes 221200 | tf_op jit(solution)/shard_map/reduce_scatter | solution.py:249
  652.5 58.2 %reduce-scatter.16.cloned.1.call-done = f32[96,6,192]{2,0,1:T(8,128)} async-done(((f32[768,6,192]{2,0,1:T(8,128)}), f32[96,6,192]{2,0,1:T(8,128)}) %reduce-scatter.16.cloned.1.call-update) | async-done | bytes 442384 | tf_op jit(solution)/shard_map/reduce_scatter | solution.py:248
  (185 shorter events, 30.6 us)
Async XLA Ops:
  7.2 36.3 %all-gather.9.cloned.1.call-start = ((), (), s32[]{:S(2)}) async-start(), calls=%async_computation.7 | async-start | bytes 2654208 | tf_op jit(solution)/shard_map/all_gather | solution.py:51
  7.9 30.8 %copy-start.1 = (bf16[3,256,768]{2,1,0:T(8,128)(2,1)S(1)}, bf16[3,256,768]{2,1,0:T(8,128)(2,1)}, u32[]{:S(2)}) copy-start(bf16[3,256,768]{2,1,0:T(8,128)(2,1)} %param.13) | copy-start | bytes 3538948
  7.9 102.3 %all-gather.17.cloned.1.call-start = ((), (), s32[]{:S(2)}) async-start(), calls=%async_computation.19 | async-start | bytes 1474560 | tf_op jit(solution)/shard_map/all_gather | solution.py:97
  36.1 7.4 %copy-start.36 = (bf16[3,768]{1,0:T(4,128)(2,1)S(1)}, bf16[3,768]{1,0:T(4,128)(2,1)}, u32[]{:S(2)}) copy-start(bf16[3,768]{1,0:T(4,128)(2,1)} %param.14) | copy-start | bytes 13828
  38.9 46.7 %copy-start.29 = (f32[3,256]{1,0:T(4,128)}, f32[3,256]{1,0:T(4,128)S(1)}, u32[]{:S(2)}) copy-start(f32[3,256]{1,0:T(4,128)S(1)} %broadcast_multiply_fusion.3) | copy-start | bytes 9220
  39.4 36.5 %copy-start.40 = (f32[3,256]{1,0:T(4,128)}, f32[3,256]{1,0:T(4,128)S(1)}, u32[]{:S(2)}) copy-start(f32[3,256]{1,0:T(4,128)S(1)} %fusion.16) | copy-start | bytes 9220
  39.4 46.2 %copy-start.39 = (f32[3,256]{1,0:T(4,128)}, f32[3,256]{1,0:T(4,128)S(1)}, u32[]{:S(2)}) copy-start(f32[3,256]{1,0:T(4,128)S(1)} %fusion.56) | copy-start | bytes 9220
  83.9 2.8 copy-start.27
  85.6 1.1 copy-start.42
  85.6 3.1 copy-start.44
  85.6 14.0 %copy-start.37 = (bf16[192,96]{1,0:T(8,128)(2,1)S(1)}, bf16[192,96]{1,0:T(8,128)(2,1)}, u32[]{:S(2)}) copy-start(bf16[192,96]{1,0:T(8,128)(2,1)} %param.19) | copy-start | bytes 110596
  86.7 1.2 copy-start.18
  88.7 38.5 %all-gather.11.cloned.1.call-start = ((), (), s32[]{:S(2)}) async-start(), calls=%async_computation.8 | async-start | bytes 1474560 | tf_op jit(solution)/shard_map/all_gather | solution.py:98
  99.5 91.3 %all-reduce.15.cloned.1.call-start = ((), (), s32[]{:S(2)}) async-start(), calls=%async_computation.9 | async-start | bytes 2359296 | tf_op jit(solution)/shard_map/psum | solution.py:116
  99.6 13.7 %copy-start.33 = (f32[3,64]{1,0:T(4,128)}, f32[3,64]{1,0:T(4,128)S(1)}, u32[]{:S(2)}) copy-start(f32[3,64]{1,0:T(4,128)S(1)} %reshape.138) | copy-start | bytes 2308
  108.9 24.2 %copy-start.14 = (bf16[192,768]{0,1:T(8,128)(2,1)}, bf16[192,768]{0,1:T(8,128)(2,1)S(1)}, u32[]{:S(2)}) copy-start(bf16[192,768]{0,1:T(8,128)(2,1)S(1)} %all_gather.51) | copy-start | bytes 884740
  110.2 5.0 copy-start.12
  113.3 3.6 copy-start
  116.9 16.1 %copy-start.21 = (f32[3,3,256]{2,1,0:T(4,128)}, f32[3,3,256]{2,1,0:T(4,128)S(1)}, u32[]{:S(2)}) copy-start(f32[3,3,256]{2,1,0:T(4,128)S(1)} %log_add_fusion) | copy-start | bytes 27652
  133.1 22.1 %copy-start.17 = (bf16[3,3,64,256]{3,2,1,0:T(8,128)(2,1)}, bf16[3,3,64,256]{3,2,1,0:T(8,128)(2,1)S(1)}, u32[]{:S(2)}) copy-start(bf16[3,3,64,256]{3,2,1,0:T(8,128)(2,1)S(1)} %convolution_convert_fusion.4) | copy-start | bytes 884740
  133.1 3.0 copy-start.43
  133.1 4.3 copy-start.46
  133.1 4.5 copy-start.47
  133.1 4.7 copy-start.48
  134.7 81.4 %all-gather.13.cloned.1.call-start = ((), (), s32[]{:S(2)}) async-start(), calls=%async_computation.10 | async-start | bytes 1327104 | tf_op jit(solution)/shard_map/all_gather | solution.py:53
  135.3 106.7 %all-gather.15.cloned.1.call-start = ((), (), s32[]{:S(2)}) async-start(), calls=%async_computation.11 | async-start | bytes 1327104 | tf_op jit(solution)/shard_map/all_gather | solution.py:55
  135.9 170.4 %all-reduce.17.cloned.1.call-start = ((), (), s32[]{:S(2)}) async-start(), calls=%async_computation.12 | async-start | bytes 2359296 | tf_op jit(solution)/shard_map/psum | solution.py:162
  190.7 2.5 copy-start.2
  194.0 0.6 copy-start.41
  216.1 25.8 %copy-start.7 = (bf16[3,256,768]{2,1,0:T(8,128)(2,1)S(1)}, bf16[3,256,768]{2,1,0:T(8,128)(2,1)}, u32[]{:S(2)}) copy-start(bf16[3,256,768]{2,1,0:T(8,128)(2,1)} %param.25) | copy-start | bytes 3538948
  242.0 6.1 copy-start.45
  247.0 1.0 copy-start.49
  250.2 97.0 %reduce-scatter.14.cloned.1.call-start = ((), (), s32[]{:S(2)}) async-start(), calls=%async_computation.14 | async-start | bytes 1474560 | tf_op jit(solution)/shard_map/reduce_scatter | solution.py:203
  306.3 3.1 copy-start.5
  308.6 2.8 copy-start.8
  308.6 2.8 copy-start.19
  308.6 2.8 copy-start.25
  308.6 2.8 copy-start.31
  309.4 4.2 copy-start.32
  311.4 2.2 copy-start.35
  311.4 3.2 copy-start.15
  311.4 3.8 copy-start.22
  313.6 1.0 copy-start.10
  315.2 6.7 copy-start.16
  321.9 53.9 %reduce-scatter.12.cloned.1.call-start = ((), (), s32[]{:S(2)}) async-start(), calls=%async_computation.13 | async-start | bytes 1474560 | tf_op jit(solution)/shard_map/reduce_scatter | solution.py:200
  322.1 7.0 copy-start.23
  329.1 5.6 copy-start.13
  329.1 5.6 copy-start.34
  334.7 2.5 copy-start.3
  337.3 138.5 %all-reduce.19.cloned.1.call-start = ((), (), s32[]{:S(2)}) async-start(), calls=%async_computation.21 | async-start | bytes 4718592 | tf_op jit(solution)/shard_map/psum | solution.py:128
  337.4 4.8 copy-start.4
  337.4 4.8 copy-start.11
  379.7 133.4 %reduce-scatter.24.cloned.1.call-start = ((), (), s32[]{:S(2)}) async-start(), calls=%async_computation.20 | async-start | bytes 884736
  382.6 196.3 %reduce-scatter.22.cloned.1.call-start = ((), (), s32[]{:S(2)}) async-start(), calls=%async_computation.18 | async-start | bytes 2654208 | tf_op jit(solution)/shard_map/reduce_scatter | solution.py:252
  387.7 218.5 %reduce-scatter.20.cloned.1.call-start = ((), (), s32[]{:S(2)}) async-start(), calls=%async_computation.17 | async-start | bytes 2654208 | tf_op jit(solution)/shard_map/reduce_scatter | solution.py:250
  392.0 260.5 %reduce-scatter.18.cloned.1.call-start = ((), (), s32[]{:S(2)}) async-start(), calls=%async_computation.16 | async-start | bytes 2654208 | tf_op jit(solution)/shard_map/reduce_scatter | solution.py:249
  397.7 312.9 %reduce-scatter.16.cloned.1.call-start = ((), (), s32[]{:S(2)}) async-start(), calls=%async_computation.15 | async-start | bytes 5308416 | tf_op jit(solution)/shard_map/reduce_scatter | solution.py:248
  475.8 2.8 copy-start.6
  475.8 2.8 copy-start.9
  475.8 2.8 copy-start.20
  475.8 2.8 copy-start.26
  475.9 2.8 copy-start.28
  475.9 2.8 copy-start.30
  478.6 6.8 copy-start.38
  (1 other events, 0.6 us)
Sparse Core Ops, SparseCore 0:
  9.9 33.5 all-gather.8
  88.8 18.5 all-gather.16
  109.5 17.5 all-gather.10
  134.8 55.8 all-reduce.14
  192.5 23.5 all-gather.12
  217.9 24.0 all-gather.14
  250.3 55.8 all-reduce.16
  322.0 25.2 reduce-scatter.13
  350.0 25.6 reduce-scatter.11
  379.8 95.9 all-reduce.18
  479.0 34.0 reduce-scatter.23
  516.8 42.4 reduce-scatter.21
  563.7 42.4 reduce-scatter.19
  610.0 42.4 reduce-scatter.17
  656.7 53.8 reduce-scatter.15
where the time goes:
time: 728 us; the launch traced here: 718 us
  waiting for transfers between devices  393 us (54%)
  blocking collectives  146 us (20%)
  matrix products  76.4 us (10%)
  other arithmetic  48.9 us (7%)
  local copies, waits for them, and re-layouts  35.6 us (5%)
  between operations  17 us (2%)
    psum x1, waiting for transfers between devices, body(): lax.psum(feed_part.astype(jnp.bfloat16), 'tensor').astype(jnp.float32)  78.1 us
    reduce_scatter x1, waiting for transfers between devices, body(): lax.psum_scatter(ada_weight_grad, ('fsdp', 'ctx'), scatter_dimension=0, t...  58.2 us
    psum x1, waiting for transfers between devices, body(): lax.psum(two_part.astype(jnp.bfloat16), 'tensor').astype(jnp.float32)  56 us
    reduce_scatter x1, waiting for transfers between devices, body(): lax.psum_scatter(qkv_weight_grad, ('fsdp', 'ctx'), scatter_dimension=0, t...  46.3 us
    unnamed x2, blocking collectives  38.4 us
    all_gather x1, blocking collectives, body(): modulation = lax.all_gather(mod_part, 'tensor', axis=2, tiled=True)  30.1 us
    psum x1, waiting for transfers between devices, body(): lax.psum(attn_part.astype(jnp.bfloat16), 'tensor').astype(jnp.float32)  29.5 us
    reduce_scatter x1, waiting for transfers between devices, body(): lax.psum_scatter(key_term.astype(jnp.bfloat16), 'ctx', scatter_dimension=...  28.5 us
  transfers between devices with their start and end apart: 15, of which 13 were waited for; matrix products, arithmetic and copies ran while one was open for 15% of the time, Pallas kernels for 0%

commit v1 on v0

v1 whole, which is shorter than its diff:
```python
import functools
import math

import jax
import jax.numpy as jnp
from jax import lax
from jax.experimental import pallas as pl
from jax.experimental.pallas import tpu as pltpu
from jax.sharding import PartitionSpec as P

HEAD_DIM = 64


EPSILON = 1e-06
GELU_SCALE = 0.7978845608028654
GELU_CUBIC = 0.044715

PLANE = ("fsdp", "ctx")
EVERY = ("fsdp", "ctx", "tensor")


def layer_norm(values):
    center = values - jnp.mean(values, axis=-1, keepdims=True)
    spread = jnp.mean(center * center, axis=-1, keepdims=True)
    return center * lax.rsqrt(spread + EPSILON)


def gelu_tanh(pre_act):
    return (
        0.5
        * pre_act
        * (1.0 + jnp.tanh(GELU_SCALE * (pre_act + GELU_CUBIC * pre_act * pre_act * pre_act)))
    )


def silu_slope(values):
    sigmoid_val = jax.nn.sigmoid(values)
    return sigmoid_val * (1.0 + values * (1.0 - sigmoid_val))


def total_of(sizes, axes):
    return math.prod(sizes[a] for a in axes)


def index_of(sizes, axes):
    me = 0
    for a in axes:
        me = me * sizes[a] + lax.axis_index(a)
    return me


def coords_of(sizes, axes, index):
    found = {}
    for a in reversed(axes):
        found[a] = lax.rem(index, sizes[a])
        index = lax.div(index, sizes[a])
    return {a: found[a] for a in axes}


def exchange_kernel(sizes, axes, cuts, *refs):
    count = len(cuts)
    ins, outs = refs[:count], refs[count : 2 * count]
    send_sem, recv_sem, own_sem = refs[2 * count :]
    n = total_of(sizes, axes)
    me = index_of(sizes, axes)

    barrier = pltpu.get_barrier_semaphore()

    def greet(step, carry):
        peer = lax.rem(me + step, n)
        pl.semaphore_signal(
            barrier,
            inc=1,
            device_id=coords_of(sizes, axes, peer),
            device_id_type=pl.DeviceIdType.MESH,
        )
        return carry

    lax.fori_loop(1, n, greet, 0)
    pl.semaphore_wait(barrier, n - 1)

    def copies(step):
        peer = lax.rem(me + step, n)
        return [
            pltpu.make_async_remote_copy(
                src_ref=cut_in(ins[i], peer),
                dst_ref=cut_out(outs[i], me),
                send_sem=send_sem.at[i, step - 1],
                recv_sem=recv_sem.at[i, step - 1],
                device_id=coords_of(sizes, axes, peer),
                device_id_type=pl.DeviceIdType.MESH,
            )
            for i, (cut_in, cut_out) in enumerate(cuts)
        ]

    def begin(step, carry):
        for copy in copies(step):
            copy.start()
        return carry

    def finish(step, carry):
        for copy in copies(step):
            copy.wait()
        return carry

    lax.fori_loop(1, n, begin, 0)
    own = [
        pltpu.make_async_copy(cut_in(ins[i], me), cut_out(outs[i], me), own_sem.at[i])
        for i, (cut_in, cut_out) in enumerate(cuts)
    ]
    for copy in own:
        copy.start()
    for copy in own:
        copy.wait()
    lax.fori_loop(1, n, finish, 0)


def whole_ref(ref, index):
    return ref


def lead(ref, index):
    return ref.at[index]


def rows(width):
    def cut(ref, index):
        return ref.at[:, pl.ds(pl.multiple_of(index * width, width), width), :]

    return cut


def exchange(sizes, axes, collective_id, items):
    n = total_of(sizes, axes)
    count = len(items)
    return pl.pallas_call(
        functools.partial(
            exchange_kernel, sizes, axes, [(item[1], item[2]) for item in items]
        ),
        out_shape=[jax.ShapeDtypeStruct(item[3], item[0].dtype) for item in items],
        in_specs=[pl.BlockSpec(memory_space=pl.ANY)] * count,
        out_specs=[pl.BlockSpec(memory_space=pl.ANY)] * count,
        scratch_shapes=[
            pltpu.SemaphoreType.DMA((count, n - 1)),
            pltpu.SemaphoreType.DMA((count, n - 1)),
            pltpu.SemaphoreType.DMA((count,)),
        ],
        compiler_params=pltpu.CompilerParams(
            collective_id=collective_id, has_side_effects=True
        ),
    )(*[item[0] for item in items])


def gather_item(x, n):
    return (x, whole_ref, lead, (n,) + x.shape)


def scatter_item(x):
    return (x, lead, lead, x.shape)


def gather_rows_item(x, n):
    return (x, whole_ref, rows(x.shape[1]), (x.shape[0], n * x.shape[1], x.shape[2]))


def scatter_rows_item(x, n):
    width = x.shape[1] // n
    return (x, rows(width), lead, (n, x.shape[0], width, x.shape[2]))


def body(
    sizes,
    latents_in,
    conditioning,
    ada_weight,
    ada_bias,
    qkv_weight,
    qv_bias,
    out_weight,
    out_bias,
    up_weight,
    up_bias,
    down_weight,
    down_bias,
    cotangent,
):
    f32, bf16 = jnp.float32, jnp.bfloat16
    n_fsdp, n_ctx, n_tensor = sizes["fsdp"], sizes["ctx"], sizes["tensor"]
    n_plane = n_fsdp * n_ctx
    plane_me = index_of(sizes, PLANE)
    fsdp_me = lax.axis_index("fsdp")
    tensor_me = lax.axis_index("tensor")
    latent_count, tok_rows, width = latents_in.shape
    own_rows = tok_rows // n_tensor
    depth = qkv_weight.shape[0]
    part = qkv_weight.shape[2]
    hid = up_weight.shape[1]
    local_heads = part // HEAD_DIM
    score_scale = 1.0 / math.sqrt(HEAD_DIM)

    def own(x):
        return lax.dynamic_slice_in_dim(x, tensor_me * own_rows, own_rows, 1)

    late_weights = jnp.concatenate([up_weight, down_weight.T, out_weight.T], axis=1)
    late_full = lax.all_gather(late_weights, PLANE, axis=0, tiled=True)

    cond = conditioning.astype(f32)
    biases = jnp.concatenate(
        [ada_bias.reshape(-1), qv_bias.reshape(-1), out_bias, up_bias, down_bias]
    )
    bias_len = biases.shape[0]
    bias_pad = -bias_len % 128
    biases = jnp.pad(biases.astype(f32), (0, bias_pad)).reshape(-1, 128)
    qkv_all, cond_all, bias_all = exchange(
        sizes,
        PLANE,
        1,
        [
            gather_item(qkv_weight.reshape(depth, 3 * part), n_plane),
            gather_item(cond, n_plane),
            gather_item(biases, n_plane),
        ],
    )
    qkv_full = qkv_all.reshape(width, 3 * part)
    bias_all = bias_all.reshape(n_plane, -1)
    piece = part // n_plane
    six = ada_bias.shape[0]
    at = 0
    ada_shift = bias_all[:, at : at + six * piece].reshape(n_plane, six, piece)
    ada_shift = ada_shift.transpose(1, 0, 2).reshape(six, part)
    at += six * piece
    qv_shift = bias_all[:, at : at + 2 * piece].reshape(n_plane, 2, piece)
    qv_shift = qv_shift.transpose(1, 0, 2).reshape(2, part)
    at += 2 * piece
    out_shift = bias_all[:, at : at + depth].reshape(width)
    at += depth
    up_piece = up_bias.shape[0]
    up_shift = bias_all[:, at : at + up_piece].reshape(hid)
    at += up_piece
    down_shift = bias_all[:, at : at + depth].reshape(width)

    cond_every = cond_all.reshape(n_fsdp, n_ctx, latent_count, width)[:, 0]
    cond_every = cond_every.reshape(n_fsdp * latent_count, width)
    cond_mine = lax.dynamic_slice_in_dim(cond_every, plane_me * depth, depth, 1)
    lifted_mine = jax.nn.silu(cond_mine).astype(bf16)
    ada_flat = ada_weight.reshape(depth, six * part)
    mod_terms = jnp.dot(lifted_mine, ada_flat, preferred_element_type=f32)
    mod_terms = mod_terms.reshape(n_fsdp, latent_count, six * part)

    def by_fsdp(ref, index):
        return ref.at[lax.div(index, n_ctx)]

    (mod_pieces,) = exchange(
        sizes,
        PLANE,
        2,
        [(mod_terms, by_fsdp, lead, (n_plane, latent_count, six * part))],
    )
    mod_part = jnp.sum(mod_pieces, axis=0) + ada_shift.reshape(1, six * part)
    (mod_all,) = exchange(sizes, ("tensor",), 3, [gather_item(mod_part, n_tensor)])
    modulation = (
        mod_all.reshape(n_tensor, latent_count, six, part)
        .transpose(1, 2, 0, 3)
        .reshape(latent_count, six, width)
    )
    shift_one, scale_one, gate_one, shift_two, scale_two, gate_two = [
        modulation[:, offset][:, None, :] for offset in range(6)
    ]

    inputs = latents_in.astype(f32)
    shifted = (layer_norm(inputs) * (1.0 + scale_one) + shift_one).astype(bf16)
    inputs_own = own(latents_in).astype(f32)
    normed_own, norm_back = jax.vjp(layer_norm, inputs_own)

    project = jnp.einsum("bld,de->ble", shifted, qkv_full, preferred_element_type=f32)
    queries = (project[:, :, :part] + qv_shift[0]).astype(bf16)
    keys_values = jnp.concatenate(
        [project[:, :, part : 2 * part], project[:, :, 2 * part :] + qv_shift[1]], axis=2
    ).astype(bf16)
    (kv_all,) = exchange(sizes, ("ctx",), 4, [gather_rows_item(keys_values, n_ctx)])
    seq_len = kv_all.shape[1]
    query_heads = queries.reshape(latent_count, tok_rows, local_heads, HEAD_DIM)
    key_heads = kv_all[:, :, :part].reshape(latent_count, seq_len, local_heads, HEAD_DIM)
    value_heads = kv_all[:, :, part:].reshape(latent_count, seq_len, local_heads, HEAD_DIM)
    scores = (
        jnp.einsum("bqhe,bkhe->bhqk", query_heads, key_heads, preferred_element_type=f32)
        * score_scale
    )
    log_total = jax.nn.logsumexp(scores, axis=-1, keepdims=True)
    prob_low = jnp.exp(scores - log_total).astype(bf16)
    mixed_heads = (
        jnp.einsum("bhqk,bkhe->bqhe", prob_low, value_heads, preferred_element_type=f32)
        .astype(bf16)
        .reshape(latent_count, tok_rows, part)
    )
    up_full = late_full[:, :hid]
    down_back = late_full[:, hid : 2 * hid]
    out_back = late_full[:, 2 * hid :]
    attn_part = jnp.einsum("bld,ed->ble", mixed_heads, out_back, preferred_element_type=f32)
    (attn_pieces,) = exchange(
        sizes, ("tensor",), 5, [scatter_rows_item(attn_part.astype(bf16), n_tensor)]
    )
    attended = jnp.sum(attn_pieces.astype(f32), axis=0) + out_shift
    after_attn = inputs_own + gate_one * attended
    normed_two, norm_back_two = jax.vjp(layer_norm, after_attn)
    shifted_two_own = (normed_two * (1.0 + scale_two) + shift_two).astype(bf16)
    (shifted_two,) = exchange(
        sizes, ("tensor",), 6, [gather_rows_item(shifted_two_own, n_tensor)]
    )
    hidden_pre = (
        jnp.einsum("bld,df->blf", shifted_two, up_full, preferred_element_type=f32) + up_shift
    )
    hidden_val, gelu_back = jax.vjp(gelu_tanh, hidden_pre)
    hidden = hidden_val.astype(bf16)
    feed_part = jnp.einsum("blf,df->bld", hidden, down_back, preferred_element_type=f32)
    feed_sum = lax.psum_scatter(
        feed_part.astype(bf16), "tensor", scatter_dimension=1, tiled=True
    )
    feed_out = feed_sum.astype(f32) + down_shift
    block_own = (after_attn + gate_two * feed_out).astype(bf16)
    block_out = lax.all_gather(block_own, "tensor", axis=1, tiled=True)

    upstream_own = own(cotangent).astype(f32)
    feed_grad = (gate_two * cotangent.astype(f32)).astype(bf16)
    gate_two_grad = jnp.sum(upstream_own * feed_out, axis=1)
    down_bias_grad = jnp.sum(feed_grad.astype(f32), axis=(0, 1))
    hidden_grad = jnp.einsum("bld,df->blf", feed_grad, down_back, preferred_element_type=f32)
    pre_grad = gelu_back(hidden_grad)[0].astype(bf16)
    two_part = jnp.einsum("blf,df->bld", pre_grad, up_full, preferred_element_type=f32)
    (two_pieces,) = exchange(
        sizes, ("tensor",), 7, [scatter_rows_item(two_part.astype(bf16), n_tensor)]
    )
    up_bias_grad = jnp.sum(pre_grad.astype(f32), axis=(0, 1))
    up_weight_grad = jnp.einsum(
        "bld,blf->df", shifted_two, pre_grad, preferred_element_type=f32
    )
    down_weight_grad = jnp.einsum("bld,blf->df", feed_grad, hidden, preferred_element_type=f32)
    feed_weights = jnp.concatenate(
        [up_weight_grad.astype(bf16), down_weight_grad.astype(bf16)], axis=1
    )
    feed_shard = lax.psum_scatter(feed_weights, PLANE, scatter_dimension=0, tiled=True)
    feed_shard = feed_shard.astype(f32)

    shifted_two_grad = jnp.sum(two_pieces.astype(f32), axis=0)
    scale_two_grad = jnp.sum(shifted_two_grad * normed_two, axis=1)
    shift_two_grad = jnp.sum(shifted_two_grad, axis=1)
    after_grad = upstream_own + norm_back_two(shifted_two_grad * (1.0 + scale_two))[0]
    attn_grad_own = (gate_one * after_grad).astype(bf16)
    gate_one_grad = jnp.sum(after_grad * attended, axis=1)
    (attn_grad,) = exchange(
        sizes, ("tensor",), 8, [gather_rows_item(attn_grad_own, n_tensor)]
    )
    out_bias_grad = jnp.sum(attn_grad.astype(f32), axis=(0, 1))
    out_weight_grad = jnp.einsum(
        "ble,bld->ed", attn_grad, mixed_heads, preferred_element_type=f32
    )
    mixed_grad = jnp.einsum(
        "ble,ed->bld", attn_grad, out_back, preferred_element_type=f32
    ).astype(bf16)
    mixed_grad = mixed_grad.reshape(latent_count, tok_rows, local_heads, HEAD_DIM)
    scores_again = (
        jnp.einsum("bqhe,bkhe->bhqk", query_heads, key_heads, preferred_element_type=f32)
        * score_scale
    )
    probs = jnp.exp(scores_again - log_total)
    prob_grad = jnp.einsum("bqhe,bkhe->bhqk", mixed_grad, value_heads, preferred_element_type=f32)
    row_term = jnp.sum(probs * prob_grad, axis=-1, keepdims=True)
    score_grad = (probs * (prob_grad - row_term)).astype(bf16)
    query_grad = (
        jnp.einsum("bhqk,bkhe->bqhe", score_grad, key_heads, preferred_element_type=f32)
        * score_scale
    ).astype(bf16)
    query_grad = query_grad.reshape(latent_count, tok_rows, part)
    probs_again = probs.astype(bf16)
    key_term = (
        jnp.einsum("bhqk,bqhe->bkhe", score_grad, query_heads, preferred_element_type=f32)
        * score_scale
    ).reshape(latent_count, seq_len, part)
    value_term = jnp.einsum(
        "bhqk,bqhe->bkhe", probs_again, mixed_grad, preferred_element_type=f32
    ).reshape(latent_count, seq_len, part)
    kv_term = jnp.concatenate([key_term.astype(bf16), value_term.astype(bf16)], axis=2)
    (kv_pieces,) = exchange(sizes, ("ctx",), 9, [scatter_rows_item(kv_term, n_ctx)])
    kv_grad = jnp.sum(kv_pieces.astype(f32), axis=0).astype(bf16)
    proj_grad = jnp.concatenate([query_grad, kv_grad], axis=2)
    proj_bias_grad = jnp.sum(proj_grad.astype(f32), axis=(0, 1)).reshape(3, part)
    one_part = jnp.einsum("ble,de->bld", proj_grad, qkv_full, preferred_element_type=f32)
    (one_pieces,) = exchange(
        sizes, ("tensor",), 10, [scatter_rows_item(one_part.astype(bf16), n_tensor)]
    )
    qkv_weight_grad = jnp.einsum("bld,ble->de", shifted, proj_grad, preferred_element_type=f32)

    shifted_grad = jnp.sum(one_pieces.astype(f32), axis=0)
    scale_one_grad = jnp.sum(shifted_grad * normed_own, axis=1)
    shift_one_grad = jnp.sum(shifted_grad, axis=1)
    grad_in_own = after_grad + norm_back(shifted_grad * (1.0 + scale_one))[0]
    mod_grad_own = jnp.stack(
        [
            shift_one_grad,
            scale_one_grad,
            gate_one_grad,
            shift_two_grad,
            scale_two_grad,
            gate_two_grad,
        ],
        axis=1,
    )
    mod_grad_own = (
        mod_grad_own.reshape(latent_count, six, n_tensor, part)
        .transpose(2, 0, 1, 3)
        .reshape(n_tensor, latent_count, six * part)
    )
    grad_in_all, mod_pieces_back = exchange(
        sizes,
        ("tensor",),
        11,
        [gather_rows_item(grad_in_own.astype(bf16), n_tensor), scatter_item(mod_grad_own)],
    )
    grad_in = grad_in_all.astype(f32)
    mod_grad_part = jnp.sum(mod_pieces_back, axis=0)

    bias_grads = jnp.concatenate(
        [
            proj_bias_grad[0].reshape(n_plane, piece),
            proj_bias_grad[2].reshape(n_plane, piece),
            out_bias_grad.reshape(n_plane, depth),
            up_bias_grad.reshape(n_plane, up_piece),
            down_bias_grad.reshape(n_plane, depth),
        ],
        axis=1,
    )
    bias_grads = jnp.pad(bias_grads, ((0, 0), (0, -bias_grads.shape[1] % 128)))
    bias_grads = bias_grads.reshape(n_plane, -1, 128)
    attn_weights = jnp.concatenate(
        [qkv_weight_grad.astype(bf16), out_weight_grad.astype(bf16)], axis=1
    ).reshape(n_plane, depth, 4 * part)
    weight_pieces, bias_pieces, mod_every = exchange(
        sizes,
        PLANE,
        12,
        [
            scatter_item(attn_weights),
            scatter_item(bias_grads),
            gather_item(mod_grad_part, n_plane),
        ],
    )
    attn_shard = jnp.sum(weight_pieces.astype(f32), axis=0)
    bias_shard = jnp.sum(bias_pieces, axis=0).reshape(-1)
    mod_grad = jnp.sum(
        mod_every.reshape(n_fsdp, n_ctx, latent_count, six * part), axis=1
    ).astype(bf16)
    mod_grad = mod_grad.reshape(n_fsdp * latent_count, six * part)
    ada_weight_grad = jnp.einsum(
        "bd,be->de", lifted_mine, mod_grad, preferred_element_type=f32
    ).reshape(depth, six, part)
    ada_bias_sum = jnp.sum(mod_grad.astype(f32), axis=0).reshape(six, part)
    ada_bias_grad = lax.dynamic_slice_in_dim(ada_bias_sum, plane_me * piece, piece, 1)
    lifted_part = jnp.einsum("be,de->bd", mod_grad, ada_flat, preferred_element_type=f32)
    (lifted_all,) = exchange(
        sizes, EVERY, 13, [gather_item(lifted_part, n_plane * n_tensor)]
    )
    lifted_grad = jnp.sum(
        lifted_all.reshape(n_plane, n_tensor, n_fsdp, latent_count, depth), axis=1
    )
    lifted_grad = lax.dynamic_index_in_dim(lifted_grad, fsdp_me, 1, keepdims=False)
    lifted_grad = lifted_grad.transpose(1, 0, 2).reshape(latent_count, width)
    grad_cond = lifted_grad * silu_slope(cond)

    at = 2 * piece
    out_bias_shard = bias_shard[at : at + depth]
    at += depth
    up_bias_shard = bias_shard[at : at + up_piece]
    at += up_piece
    down_bias_shard = bias_shard[at : at + depth]
    return (
        block_out,
        grad_in,
        grad_cond,
        ada_weight_grad,
        ada_bias_grad,
        attn_shard[:, : 3 * part].reshape(depth, 3, part),
        bias_shard[: 2 * piece].reshape(2, piece),
        attn_shard[:, 3 * part :].T,
        out_bias_shard,
        feed_shard[:, :hid],
        up_bias_shard,
        feed_shard[:, hid:].T,
        down_bias_shard,
    )


def solution(mesh):
    in_specs = (
        P("fsdp", "ctx", None),
        P("fsdp", None),
        P(("fsdp", "ctx"), None, "tensor"),
        P(None, ("tensor", "fsdp", "ctx")),
        P(("fsdp", "ctx"), None, "tensor"),
        P(None, ("tensor", "fsdp", "ctx")),
        P("tensor", ("fsdp", "ctx")),
        P(("fsdp", "ctx")),
        P(("fsdp", "ctx"), "tensor"),
        P(("tensor", "fsdp", "ctx")),
        P("tensor", ("fsdp", "ctx")),
        P(("fsdp", "ctx")),
        P("fsdp", "ctx", None),
    )
    out_specs = (
        P("fsdp", "ctx", None),
        P("fsdp", "ctx", None),
        P("fsdp", None),
        P(("fsdp", "ctx"), None, "tensor"),
        P(None, ("tensor", "fsdp", "ctx")),
        P(("fsdp", "ctx"), None, "tensor"),
        P(None, ("tensor", "fsdp", "ctx")),
        P("tensor", ("fsdp", "ctx")),
        P(("fsdp", "ctx")),
        P(("fsdp", "ctx"), "tensor"),
        P(("tensor", "fsdp", "ctx")),
        P("tensor", ("fsdp", "ctx")),
        P(("fsdp", "ctx")),
    )
    return jax.shard_map(functools.partial(body, dict(mesh.shape)), mesh=mesh, in_specs=in_specs, out_specs=out_specs, check_vma=False)
```

time: 728 us -> 499 us (0.69)
  waiting for transfers between devices: 393 us -> 10.7 us
  Pallas kernels: 0 us -> 299 us
  blocking collectives: 146 us -> 0 us
  local copies, waits for them, and re-layouts: 35.6 us -> 66.8 us
  matrix products: 76.4 us -> 48.5 us
    pallas_call x0 -> x13, Pallas kernels: none -> 299 us  [exchange(): pl.pallas_call(functools.partial(exchange_kernel, sizes, axes, [(item[1],...]
    psum x3 -> x0, waiting for transfers between devices: 164 us -> none  [the longest x1 78.1 us: body(): lax.psum(feed_part.astype(jnp.bfloat16), 'tensor').astype(jnp.float32)]
    reduce_scatter x6 -> x1, waiting for transfers between devices: 162 us -> 0.02 us  [body(): lax.psum_scatter(feed_part.astype(bf16), 'tensor', scatter_dimension=1, t...]
    all_gather x5 -> x0, blocking collectives: 75 us -> none  [the longest x1 30.1 us: body(): modulation = lax.all_gather(mod_part, 'tensor', axis=2, tiled=True)]
    all_gather x5 -> x2, waiting for transfers between devices: 56.8 us -> 10.6 us  [the longest x1 10.6 us: body(): block_out = lax.all_gather(block_own, 'tensor', axis=1, tiled=True)]
    unnamed x2 -> x0, blocking collectives: 38.4 us -> none
    psum x2 -> x0, blocking collectives: 32.5 us -> none  [the longest x1 19.9 us: body(): lifted_grad = lax.psum(lifted_part, 'tensor')]
    dot_general x15, matrix products: 48.5 us -> 32.4 us  [the longest x1 5.17 us: body(): jnp.einsum('bld,df->blf', feed_grad, down_back, preferred_element_type=f32)]
  transfers between devices with their start and end apart: 15 -> 4, of which waited for: 13 -> 1; matrix products, arithmetic and copies ran while one was open for 15% -> 28% of each run, Pallas kernels for 0% -> 50%
where the time goes in v1:
time: 499 us; the launch traced here: 490 us
  Pallas kernels  299 us (60%)
  local copies, waits for them, and re-layouts  66.8 us (13%)
  other arithmetic  49.2 us (10%)
  matrix products  48.5 us (10%)
  between operations  15.2 us (3%)
  waiting for transfers between devices  10.7 us (2%)
    pallas_call x13, Pallas kernels, exchange(): pl.pallas_call(functools.partial(exchange_kernel, sizes, axes, [(item[1],...  299 us
    unnamed x124, local copies, waits for them, and re-layouts  27.2 us
    all_gather x1, waiting for transfers between devices, body(): block_out = lax.all_gather(block_own, 'tensor', axis=1, tiled=True)  10.6 us
  transfers between devices with their start and end apart: 4, of which 1 were waited for; matrix products, arithmetic and copies ran while one was open for 28% of the time, Pallas kernels for 50%

profile of v1, /device:TPU:0, one launch (start us, length us, event | category | flops | bytes accessed | tf_op | source)
XLA Modules:
  0.0 489.7 jit_solution(6683868064658880740)
XLA Ops:
  8.2 1.7 pad_maximum_fusion.5
  14.7 2.1 concatenate.26
  17.4 19.9 %shard_map.228 = (bf16[8,96,576]{2,1,0:T(8,128)(2,1)}, f32[8,3,768]{2,1,0:T(4,128)}, f32[8,4,128]{2,1,0:T(4,128)}) custom-call(bf16[96,576]{1,0:T(8,128)(2,1)} %copy.147.refs_0_, f32[3,768]{1,0:T(4,128)} %convert_element_type.170.refs_1_, f32[4,128]{1,0:T(4,128)} %bitcast_convert_fusion.3.refs_2_), custom_call_target="tpu_custom_call" | custom-call | tf_op jit(solution)/shard_map/pallas_call | solution.py:136
  41.5 7.8 %shard_map.229 = f32[8,3,1152]{2,1,0:T(4,128)} custom-call(f32[2,3,1152]{2,1,0:T(4,128)} %fusion.48.refs_0_), custom_call_target="tpu_custom_call" | custom-call | tf_op jit(solution)/shard_map/pallas_call | solution.py:136
  51.0 7.0 %shard_map.230 = f32[4,3,1152]{2,1,0:T(4,128)} custom-call(f32[3,1152]{1,0:T(4,128)} %broadcast_add_fusion.refs_0_), custom_call_target="tpu_custom_call" | custom-call | tf_op jit(solution)/shard_map/pallas_call | solution.py:136
  65.8 28.2 %shard_map.231 = bf16[3,1024,384]{2,1,0:T(8,128)(2,1)} custom-call(bf16[3,256,384]{2,1,0:T(8,128)(2,1)} %pad_maximum_fusion.4.refs_0_), custom_call_target="tpu_custom_call" | custom-call | tf_op jit(solution)/shard_map/pallas_call | solution.py:136
  94.0 4.3 fusion.43
  98.3 1.7 copy.158
  100.1 1.7 copy.157
  105.2 1.4 add.210
  108.0 2.1 convert_reduce_fusion.6
  110.1 1.3 reshape.284
  111.5 2.5 multiply_reduce_fusion.1
  114.0 1.9 exponential_reduce_fusion
  115.9 1.6 copy-done
  117.6 2.8 convolution_convert_fusion.5
  120.4 2.6 convolution_convert_fusion.3.refs_0_
  123.0 24.5 %shard_map.232 = bf16[4,3,64,768]{3,2,1,0:T(8,128)(2,1)} custom-call(bf16[3,256,768]{2,1,0:T(8,128)(2,1)} %convolution_convert_fusion.3.refs_0_), custom_call_target="tpu_custom_call" | custom-call | tf_op jit(solution)/shard_map/pallas_call | solution.py:136
  147.5 1.5 convert_reduce_fusion.9
  151.8 29.2 %shard_map.233 = bf16[3,256,768]{2,1,0:T(8,128)(2,1)} custom-call(bf16[3,64,768]{2,1,0:T(8,128)(2,1)} %add_convert_fusion.3.refs_0_), custom_call_target="tpu_custom_call" | custom-call | tf_op jit(solution)/shard_map/pallas_call | solution.py:136
  181.0 2.7 fusion.15
  183.8 1.4 copy-done.44
  185.2 3.9 convolution_convert_fusion.2
  189.2 5.2 %convert_reduce_fusion.7 = (f32[768]{0:T(1024)S(1)}, bf16[3,256,768]{2,1,0:T(8,128)(2,1)S(1)}) fusion(bf16[768,1728]{1,0:T(8,128)(2,1)} %all-gather.3.cloned.1.call-done, bf16[3,256,768]{2,1,0:T(8,128)(2,1)} %param.25, f32[3,768]{1,0:T(4,128)S(1)} %bitcast.165, f32[3,256,768]{2,1,0:T(8,128)} %copy-done.44, f32[768]{0:T(1024)S(1)} %copy-done.42), kind=kOutput, calls=%fused_computation.34 | convolution fusion | flops 923663616 | bytes 5913600 | tf_op jit(solution)/shard_map/bld,df->blf/dot_general | solution.py:327
  196.9 1.6 bitcast_convert_fusion
  198.5 1.6 pad_maximum_fusion.1
  200.1 4.3 copy.188
  204.4 3.8 convolution_convert_fusion.1.refs_0_
  208.1 33.1 %shard_map.234 = bf16[4,3,64,768]{3,2,1,0:T(8,128)(2,1)} custom-call(bf16[3,256,768]{2,1,0:T(8,128)(2,1)} %convolution_convert_fusion.1.refs_0_), custom_call_target="tpu_custom_call" | custom-call | tf_op jit(solution)/shard_map/pallas_call | solution.py:136
  241.9 2.2 convert_reduce_fusion.2
  244.1 1.4 stack.24
  245.5 1.6 multiply_reduce_fusion.2
  247.1 1.4 stack.25
  251.1 2.0 fusion.41
  253.9 1.8 multiply_convert_fusion.6.refs_0_
  255.7 29.2 %shard_map.235 = bf16[3,256,768]{2,1,0:T(8,128)(2,1)} custom-call(bf16[3,64,768]{2,1,0:T(8,128)(2,1)} %multiply_convert_fusion.6.refs_0_), custom_call_target="tpu_custom_call" | custom-call | tf_op jit(solution)/shard_map/pallas_call | solution.py:136
  285.0 2.0 convolution_convert_fusion.6
  287.0 5.7 %multiply_reduce_fusion = (f32[3,3,256]{2,1,0:T(4,128)S(1)}, f32[3,3,256,1024]{3,2,1,0:T(8,128)S(1)}) fusion(f32[3,3,256,1024]{3,2,1,0:T(8,128)} %copy-done, f32[3,3,256]{2,1,0:T(4,128)S(1)} %log_add_fusion, bf16[3,256,3,64]{1,3,2,0:T(8,128)(2,1)S(1)} %bitcast.143, bf16[3,1024,3,64]{1,3,2,0:T(8,128)(2,1)S(1)} %bitcast.139), kind=kOutput, calls=%fused_computation.1 | convolution fusion | flops 311424768 | bytes 20367360 | tf_op jit(solution)/shard_map/bqhe,bkhe->bhqk/dot_general | solution.py:366
  293.6 2.3 multiply_convert_fusion
  295.9 2.3 fusion.13
  299.2 1.8 convolution_convert_fusion
  301.0 1.6 copy.161
  302.6 1.5 copy.162
  304.1 4.1 pad_maximum_fusion.refs_0_
  308.3 27.7 %shard_map.236 = bf16[4,3,256,384]{3,2,1,0:T(8,128)(2,1)} custom-call(bf16[3,1024,384]{2,1,0:T(8,128)(2,1)} %pad_maximum_fusion.refs_0_), custom_call_target="tpu_custom_call" | custom-call | tf_op jit(solution)/shard_map/pallas_call | solution.py:136
  336.0 3.1 reduce_sum.327
  341.2 1.4 reshape_squeeze.10
  342.6 1.4 reshape_squeeze.11
  344.7 1.4 reshape.282
  346.1 1.4 concatenate.32
  349.2 1.8 bitcast_convert_fusion.2
  351.1 1.5 copy.167
  352.6 3.4 convolution_convert_fusion.4.refs_0_
  355.9 29.3 %shard_map.237 = bf16[4,3,64,768]{3,2,1,0:T(8,128)(2,1)} custom-call(bf16[3,256,768]{2,1,0:T(8,128)(2,1)} %convolution_convert_fusion.4.refs_0_), custom_call_target="tpu_custom_call" | custom-call | tf_op jit(solution)/shard_map/pallas_call | solution.py:136
  385.3 1.7 convert_reduce_fusion
  387.9 2.2 fusion.25
  391.1 30.1 %shard_map.238 = (bf16[3,256,768]{2,1,0:T(8,128)(2,1)}, f32[4,3,1152]{2,1,0:T(4,128)}) custom-call(bf16[3,64,768]{2,1,0:T(8,128)(2,1)} %get-tuple-element.114.refs_0_, f32[4,3,1152]{2,1,0:T(4,128)} %reshape.305.refs_1_), custom_call_target="tpu_custom_call" | custom-call | tf_op jit(solution)/shard_map/pallas_call | solution.py:136
  421.2 1.5 reduce_sum.343.refs_2_
  422.8 17.2 %shard_map.239 = (bf16[8,96,768]{2,1,0:T(8,128)(2,1)}, f32[8,3,128]{2,1,0:T(4,128)}, f32[8,3,1152]{2,1,0:T(4,128)}) custom-call(bf16[8,96,768]{2,1,0:T(8,128)(2,1)} %bitcast.141, f32[8,3,128]{2,1,0:T(4,128)} %copy.168.refs_1_, f32[3,1152]{1,0:T(4,128)} %reduce_sum.343.refs_2_), custom_call_target="tpu_custom_call" | custom-call | tf_op jit(solution)/shard_map/pallas_call | solution.py:136
  440.0 1.6 convert_reduce_fusion.5
  444.4 15.9 %shard_map.240 = f32[32,6,96]{2,1,0:T(8,128)} custom-call(f32[6,96]{1,0:T(8,128)} %fusion.49.refs_0_), custom_call_target="tpu_custom_call" | custom-call | tf_op jit(solution)/shard_map/pallas_call | solution.py:136
  462.1 1.6 convert_element_type.205
  469.8 10.6 %all-gather.5.cloned.1.call-done = bf16[3,256,768]{2,1,0:T(8,128)(2,1)} async-done(((bf16[3,64,768]{2,1,0:T(8,128)(2,1)}), bf16[3,256,768]{2,1,0:T(8,128)(2,1)}) %all-gather.5.cloned.1.call-update) | async-done | bytes 1179664 | tf_op jit(solution)/shard_map/all_gather | solution.py:321
  480.4 2.4 copy.220
  (223 shorter events, 53.2 us)
Async XLA Ops:
  7.2 52.0 %copy-start.2 = (bf16[3,256,768]{2,1,0:T(8,128)(2,1)S(1)}, bf16[3,256,768]{2,1,0:T(8,128)(2,1)}, u32[]{:S(2)}) copy-start(bf16[3,256,768]{2,1,0:T(8,128)(2,1)} %param.13) | copy-start | bytes 3538948
  7.2 113.2 %all-gather.3.cloned.1.call-start = ((), (), s32[]{:S(2)}) async-start(), calls=%async_computation.2 | async-start | bytes 3096576 | tf_op jit(solution)/shard_map/all_gather | solution.py:205
  10.0 241.1 %reduce-scatter.5.cloned.1.call-start = ((), (), s32[]{:S(2)}) async-start(), calls=%async_computation.3 | async-start | bytes 1474560 | tf_op jit(solution)/shard_map/reduce_scatter | solution.py:316
  38.9 0.5 copy-start.36
  39.5 22.5 %copy-start.43 = (bf16[8,96,576]{2,1,0:T(8,128)(2,1)S(1)}, bf16[8,96,576]{2,1,0:T(8,128)(2,1)}, u32[]{:S(2)}) copy-start(bf16[8,96,576]{2,1,0:T(8,128)(2,1)} %get-tuple-element.23) | copy-start | bytes 2654212
  40.7 22.6 %copy-start.11 = (bf16[96,6,192]{0,2,1:T(8,128)(2,1)}, bf16[96,6,192]{0,2,1:T(8,128)(2,1)S(1)}, u32[]{:S(2)}) copy-start(bf16[96,6,192]{0,2,1:T(8,128)(2,1)S(1)} %copy.149) | copy-start | bytes 663556
  59.4 3.8 copy-start.38
  59.9 3.4 copy-start.41
  61.4 1.9 copy-start.18
  62.0 1.3 copy-start.40
  101.8 14.1 %copy-start.3 = (bf16[3,1024,192]{1,2,0:T(8,128)(2,1)}, bf16[3,1024,192]{1,2,0:T(8,128)(2,1)S(1)}, u32[]{:S(2)}) copy-start(bf16[3,1024,192]{1,2,0:T(8,128)(2,1)S(1)} %copy.157) | copy-start | bytes 3538948
  104.5 44.5 %copy-start.29 = (f32[768]{0:T(1024)}, f32[768]{0:T(1024)S(1)}, u32[]{:S(2)}) copy-start(f32[768]{0:T(1024)S(1)} %add.201) | copy-start | bytes 9220
  105.2 8.7 %copy-start.24 = (f32[3,1,768]{2,0,1:T(4,128)}, f32[3,1,768]{2,0,1:T(4,128)S(1)}, u32[]{:S(2)}) copy-start(f32[3,1,768]{2,0,1:T(4,128)S(1)} %copy.212) | copy-start | bytes 27652
  113.9 3.6 copy-start
  123.0 26.9 %copy-start.22 = (f32[3,1,768]{2,0,1:T(4,128)S(1)}, f32[3,1,768]{2,0,1:T(4,128)}, u32[]{:S(2)}) copy-start(f32[3,1,768]{2,0,1:T(4,128)} %copy.213) | copy-start | bytes 27652
  147.5 3.4 copy-start.20
  147.5 3.4 copy-start.26
  149.0 0.8 copy-start.5
  150.8 32.9 %copy-start.35 = (f32[3,64]{1,0:T(4,128)}, f32[3,64]{1,0:T(4,128)S(1)}, u32[]{:S(2)}) copy-start(f32[3,64]{1,0:T(4,128)S(1)} %multiply_reduce_fusion.5) | copy-start | bytes 2308
  150.9 32.9 %copy-start.32 = (f32[3,64]{1,0:T(4,128)}, f32[3,64]{1,0:T(4,128)S(1)}, u32[]{:S(2)}) copy-start(f32[3,64]{1,0:T(4,128)S(1)} %fusion.35) | copy-start | bytes 2308
  181.0 4.2 copy-start.42
  183.8 1.4 copy-start.44
  185.2 4.0 copy-start.25
  189.2 277.6 %reduce-scatter.7.cloned.1.call-start = ((), (), s32[]{:S(2)}) async-start(), calls=%async_computation.5 | async-start | bytes 2654208
  189.2 5.2 %copy-start.17 = (bf16[3,256,768]{2,1,0:T(8,128)(2,1)S(1)}, bf16[3,256,768]{2,1,0:T(8,128)(2,1)}, u32[]{:S(2)}) copy-start(bf16[3,256,768]{2,1,0:T(8,128)(2,1)} %shard_map.233) | copy-start | bytes 3538948
  194.4 1.2 copy-start.46
  194.4 1.7 copy-start.13
  194.4 2.4 copy-start.45
  251.0 229.4 %all-gather.5.cloned.1.call-start = ((), (), s32[]{:S(2)}) async-start(), calls=%async_computation.4 | async-start | bytes 1474560 | tf_op jit(solution)/shard_map/all_gather | solution.py:321
  251.0 2.8 copy-start.23
  253.0 0.8 copy-start.7
  253.0 33.9 %copy-start.4 = (bf16[3,1024,192]{1,2,0:T(8,128)(2,1)S(1)}, bf16[3,1024,192]{1,2,0:T(8,128)(2,1)}, u32[]{:S(2)}) copy-start(bf16[3,1024,192]{1,2,0:T(8,128)(2,1)} %copy-done.3) | copy-start | bytes 3538948
  286.9 5.8 %slice-start = ((s8[9437184]{0:T(1024)(128)(4,1)}), s8[4194304]{0:T(1024)(128)(4,1)S(1)}, s32[]{:S(2)}) async-start(s8[9437184]{0:T(1024)(128)(4,1)} %bitcast.134), calls=%async_computation.6 | async-start | bytes 8388608
  286.9 6.4 %slice-start.1 = ((s8[9437184]{0:T(1024)(128)(4,1)}), s8[4194304]{0:T(1024)(128)(4,1)S(1)}, s32[]{:S(2)}) async-start(s8[9437184]{0:T(1024)(128)(4,1)} %bitcast.134), calls=%async_computation.7 | async-start | bytes 8388608
  286.9 6.6 %slice-start.2 = ((s8[9437184]{0:T(1024)(128)(4,1)}), s8[1048576]{0:T(1024)(128)(4,1)S(1)}, s32[]{:S(2)}) async-start(s8[9437184]{0:T(1024)(128)(4,1)} %bitcast.134), calls=%async_computation.8 | async-start | bytes 2097152
  295.9 2.3 copy-start.9
  336.0 4.5 copy-start.14
  336.0 8.0 %copy-start.1 = (bf16[3,256,768]{2,1,0:T(8,128)(2,1)S(1)}, bf16[3,256,768]{2,1,0:T(8,128)(2,1)}, u32[]{:S(2)}) copy-start(bf16[3,256,768]{2,1,0:T(8,128)(2,1)} %shard_map.235) | copy-start | bytes 3538948
  339.1 9.7 %copy-start.10 = (bf16[3,3,64,256]{3,2,1,0:T(8,128)(2,1)S(1)}, bf16[3,3,64,256]{3,2,1,0:T(8,128)(2,1)}, u32[]{:S(2)}) copy-start(bf16[3,3,64,256]{3,2,1,0:T(8,128)(2,1)} %convolution_convert_fusion.5) | copy-start | bytes 884740
  339.1 10.2 %copy-start.19 = (f32[3,768]{1,0:T(4,128)S(1)}, f32[3,768]{1,0:T(4,128)}, u32[]{:S(2)}) copy-start(f32[3,768]{1,0:T(4,128)} %copy-done.18) | copy-start | bytes 27652
  355.9 31.2 %copy-start.33 = (f32[3,64]{1,0:T(4,128)S(1)}, f32[3,64]{1,0:T(4,128)}, u32[]{:S(2)}) copy-start(f32[3,64]{1,0:T(4,128)} %broadcast_multiply_fusion.1) | copy-start | bytes 2308
  385.3 2.6 copy-start.6
  385.3 2.6 copy-start.8
  385.3 2.6 copy-start.16
  385.3 2.6 copy-start.30
  385.3 2.6 copy-start.31
  387.1 3.2 copy-start.27
  387.1 3.2 copy-start.28
  422.8 20.9 %copy-start.12 = (bf16[96,6,192]{0,2,1:T(8,128)(2,1)S(1)}, bf16[96,6,192]{0,2,1:T(8,128)(2,1)}, u32[]{:S(2)}) copy-start(bf16[96,6,192]{0,2,1:T(8,128)(2,1)} %copy-done.11) | copy-start | bytes 663556
  439.9 2.7 copy-start.21
  439.9 21.5 %copy-start.39 = (f32[8,3,128]{2,1,0:T(4,128)S(1)}, f32[8,3,128]{2,1,0:T(4,128)}, u32[]{:S(2)}) copy-start(f32[8,3,128]{2,1,0:T(4,128)} %get-tuple-element.28) | copy-start | bytes 36868
  440.0 22.2 %copy-start.15 = (bf16[3,256,768]{2,1,0:T(8,128)(2,1)S(1)}, bf16[3,256,768]{2,1,0:T(8,128)(2,1)}, u32[]{:S(2)}) copy-start(bf16[3,256,768]{2,1,0:T(8,128)(2,1)} %get-tuple-element.24) | copy-start | bytes 3538948
  442.8 22.2 %copy-start.34 = (bf16[3,768]{1,0:T(4,128)(2,1)S(1)}, bf16[3,768]{1,0:T(4,128)(2,1)}, u32[]{:S(2)}) copy-start(bf16[3,768]{1,0:T(4,128)(2,1)} %param.14) | copy-start | bytes 13828
  442.8 22.8 %copy-start.37 = (bf16[6,96]{1,0:T(8,128)(2,1)S(1)}, bf16[6,96]{1,0:T(8,128)(2,1)}, u32[]{:S(2)}) copy-start(bf16[6,96]{1,0:T(8,128)(2,1)} %copy-done.36) | copy-start | bytes 3460
Sparse Core Ops, SparseCore 0:
  10.5 43.3 all-gather.2
  189.3 41.5 reduce-scatter.4
  251.1 47.6 reduce-scatter.6
  442.9 37.4 all-gather.4
